TPU v7x, 32 devices: a whole 2x2x4 slice. The times are simulated.
32 devices in a mesh: req: 4 (over x, core), tp: 8 (over z, y).
Axes of the slice: x: 2, y: 2, z: 4, core: 2. Of those that a mesh axis runs over, the one named last changes fastest.
Arguments:
- tokens: bfloat16 [4, 256, 3200], P('req', 'tp'), may hold values from -6 to 6
- segments: int32 [4, 256], P('req'), may hold values from -1 to 3, as said below
- norm_gain: float32 [3200], replicated, may hold values from 0.25 to 1.75
- wqkv: bfloat16 [3, 3200, 2048], P(None, None, 'tp'), may hold values from -4 to 4
- qk_gain: float32 [2, 2048], P(None, 'tp'), may hold values from 0.6 to 4
- wproj: bfloat16 [2048, 3200], P('tp'), may hold values from -0.125 to 0.125
- bproj: float32 [3200], P('tp'), may hold values from -3 to 3
- layer_scale: float32 [3200], P('tp'), may hold values from 0.3 to 1.5
- ln_weight: float32 [4, 3200], P(None, 'tp'), may hold values from 0.25 to 1.75
- ln_bias: float32 [4, 3200], P(None, 'tp'), may hold values from -2 to 2
- w_merge: bfloat16 [4, 3200, 3072], P(None, 'tp'), may hold values from -0.0546875 to 0.0546875
- b_merge: float32 [3072], replicated, may hold values from -3 to 3
- owners: int32 [4, 64, 1], P(None, 'tp'), may hold values from 0 to 3; in each aligned block of 8 rows (0 to 7, 8 to 15, ..., all dimensions but the last counted through in order) at most 3 rows name the same one
Outputs:
- lm_inputs: bfloat16 [4, 4, 8, 3, 3072], P('req', None, 'tp')
Inputs may be any that keep to these rules, and one draw needn't show every extreme that they name: `segments`: each group's tokens are whole images, each a whole number of blocks of 64 tokens (two patch rows); image numbers start at 0 and never fall; padding tokens (-1) fill the end of a group from a block boundary; some group has no padding and some group has padding. `owners`: among the 8 merged tokens of one device (aligned blocks of one group), at most 3 name the same owner.
All inputs are finite; a program needn't handle non-finite values.
Results may differ from a plain program's by a relative error of at most 0.014.
Values may be sent and summed in bfloat16 or wider, within the bound.
A program may use at most 64 MiB of HBM per device.

v0:
```python
import jax
import jax.numpy as jnp
from jax import lax
from jax.sharding import PartitionSpec as P

D = 3200
HEADS = 16
HD = 128
PW = 32


EPS_RMS = 1e-06
EPS_LN = 1e-05


def block_count(length):
    number = max(1, length // 512)
    while length % number:
        number = number - 1
    return number


def attend_block(query_rows, key_heads, value_heads, query_segs, key_segs):
    scores = jnp.einsum(
        "hqd,hkd->hqk", query_rows, key_heads, preferred_element_type=jnp.float32
    ) * HD ** (-0.5)
    same_image = query_segs[:, None] == key_segs[None, :]
    scores = jnp.where(same_image[None], scores, -jnp.inf)
    row_max = jnp.max(scores, axis=-1, keepdims=True)
    weights = jnp.exp(scores - row_max)
    probabilities = (weights / jnp.sum(weights, axis=-1, keepdims=True)).astype(jnp.bfloat16)
    mixed = jnp.einsum(
        "hqk,hkd->hqd", probabilities, value_heads, preferred_element_type=jnp.float32
    )
    return mixed.astype(jnp.bfloat16)


def merge_rows(stream):
    feature_count = stream.shape[-1]
    shaped = stream.reshape(stream.shape[0] // (2 * PW), 2, PW // 2, 2, feature_count)
    return shaped.transpose(0, 2, 1, 3, 4).reshape(stream.shape[0] // 4, 4, feature_count)


def slot_ranks(owner_ids, group_total):
    owner_hits = (owner_ids[:, None] == jnp.arange(group_total, dtype=jnp.int32)[None, :]).astype(
        jnp.int32
    )
    before = jnp.cumsum(owner_hits, axis=0) - owner_hits
    return jnp.sum(before * owner_hits, axis=1)


def per_device(
    tokens,
    segments,
    norm_gain,
    wqkv,
    qk_gain,
    wproj,
    bproj,
    layer_scale,
    ln_weight,
    ln_bias,
    w_merge,
    b_merge,
    owners,
):
    tp_total = lax.axis_size("tp")
    tp_index = lax.axis_index("tp")
    req_index = lax.axis_index("req")
    group_total = lax.axis_size("req")
    gathered = lax.all_gather(tokens, "tp", axis=1, tiled=True)[0]
    seq_len = gathered.shape[0]
    group_segs = segments[0]
    widened = gathered.astype(jnp.float32)
    normed = (
        widened
        * lax.rsqrt(jnp.mean(widened * widened, axis=-1, keepdims=True) + EPS_RMS)
        * norm_gain
    ).astype(jnp.bfloat16)
    proj_qkv = jnp.einsum("td,ide->ite", normed, wqkv, preferred_element_type=jnp.float32)
    q_part = proj_qkv[0]
    k_part = proj_qkv[1]
    v_part = proj_qkv[2]
    square_sums = lax.psum(
        (jnp.sum(q_part * q_part, axis=-1), jnp.sum(k_part * k_part, axis=-1)), "tp"
    )
    inner_width = HEADS * HD
    q_scaled = (
        q_part * lax.rsqrt(square_sums[0] / inner_width + EPS_RMS)[:, None] * qk_gain[0]
    ).astype(jnp.bfloat16)
    k_scaled = (
        k_part * lax.rsqrt(square_sums[1] / inner_width + EPS_RMS)[:, None] * qk_gain[1]
    ).astype(jnp.bfloat16)
    v_scaled = v_part.astype(jnp.bfloat16)
    heads_here = q_part.shape[1] // HD

    def split_heads(matrix):
        return matrix.reshape(seq_len, heads_here, HD).transpose(1, 0, 2)

    block_total = block_count(seq_len)
    block_rows = seq_len // block_total
    query_blocks = (
        split_heads(q_scaled).reshape(heads_here, block_total, block_rows, HD).transpose(1, 0, 2, 3)
    )
    seg_blocks = group_segs.reshape(block_total, block_rows)
    key_heads = split_heads(k_scaled)
    value_heads = split_heads(v_scaled)
    mixed = lax.map(
        lambda block_item: attend_block(
            block_item[0], key_heads, value_heads, block_item[1], group_segs
        ),
        (query_blocks, seg_blocks),
    )
    attended = mixed.transpose(0, 2, 1, 3).reshape(seq_len, heads_here * HD)
    width_dev = bproj.shape[0]
    head_part = jnp.dot(attended, wproj, preferred_element_type=jnp.float32)
    attn_out = lax.psum_scatter(head_part, "tp", scatter_dimension=1, tiled=True)
    own_columns = lax.dynamic_slice_in_dim(gathered, tp_index * width_dev, width_dev, 1).astype(
        jnp.float32
    )
    stream = (own_columns + layer_scale * (attn_out + bproj)).astype(jnp.bfloat16)
    merged = merge_rows(stream).astype(jnp.float32)
    feature_total = 4 * D
    row_mean = lax.psum(jnp.sum(merged, axis=(1, 2)), "tp") / feature_total
    centered = merged - row_mean[:, None, None]
    row_var = lax.psum(jnp.sum(centered * centered, axis=(1, 2)), "tp") / feature_total
    normal_rows = (
        centered * lax.rsqrt(row_var + EPS_LN)[:, None, None] * ln_weight + ln_bias
    ).astype(jnp.bfloat16)
    merged_total = normal_rows.shape[0]
    flat_rows = normal_rows.reshape(merged_total, 4 * width_dev)
    flat_weight = w_merge.reshape(4 * width_dev, w_merge.shape[2])
    merged_dev = merged_total // tp_total
    own_rows = lax.psum_scatter(
        jnp.dot(flat_rows, flat_weight, preferred_element_type=jnp.float32),
        "tp",
        scatter_dimension=0,
        tiled=True,
    )
    first_tokens = merge_rows(group_segs.reshape(seq_len, 1))[:, 0, 0]
    own_first = lax.dynamic_slice_in_dim(first_tokens, tp_index * merged_dev, merged_dev, 0)
    live_rows = (own_first >= 0).astype(jnp.float32)
    out_rows = (jax.nn.gelu(own_rows + b_merge, approximate=False) * live_rows[:, None]).astype(
        jnp.bfloat16
    )
    capacity = (merged_dev + group_total - 1) // group_total + 1
    group_ids = jnp.arange(group_total, dtype=jnp.int32)
    slot_ids = jnp.arange(capacity, dtype=jnp.int32)
    mine_ids = lax.dynamic_index_in_dim(owners[:, :, 0], req_index, 0, keepdims=False)
    slot_rank = slot_ranks(mine_ids, group_total)
    selector = (mine_ids[None, None, :] == group_ids[:, None, None]) & (
        slot_rank[None, None, :] == slot_ids[None, :, None]
    )
    outgoing = jnp.einsum(
        "gcm,mf->gcf", selector.astype(jnp.bfloat16), out_rows, preferred_element_type=jnp.float32
    ).astype(jnp.bfloat16)
    incoming = lax.all_to_all(outgoing, "req", split_axis=0, concat_axis=0, tiled=True)
    return incoming.reshape(1, group_total, 1, capacity, incoming.shape[-1])


def solution(mesh):
    placed = (
        P("req", "tp", None),
        P("req", None),
        P(),
        P(None, None, "tp"),
        P(None, "tp"),
        P("tp", None),
        P("tp"),
        P("tp"),
        P(None, "tp"),
        P(None, "tp"),
        P(None, "tp", None),
        P(),
        P(None, "tp", None),
    )
    return jax.shard_map(
        per_device,
        mesh=mesh,
        in_specs=placed,
        out_specs=P("req", None, "tp", None, None),
        check_vma=False,
    )
```

profile of v0, /device:TPU:0, one launch (start us, length us, event | category | flops | bytes accessed | tf_op | source)
XLA Modules:
  0.0 283.3 jit_solution(1449557033337712268)
XLA Ops:
  6.5 0.0 copy-start
  6.5 0.0 all-gather.2.cloned.1.call-start
  6.5 0.7 all-gather.2.cloned.1.call-update
  7.3 0.0 reduce-scatter.3.cloned.1.call-start
  7.3 0.8 fusion.80
  8.1 0.9 broadcast_compare_fusion
  8.9 47.9 %all-gather.2.cloned.1.call-done = bf16[1,256,3200]{2,1,0:T(8,128)(2,1)} async-done(((bf16[1,32,3200]{2,1,0:T(8,128)(2,1)}), bf16[1,256,3200]{2,1,0:T(8,128)(2,1)}) %all-gather.2.cloned.1.call-update) | async-done | bytes 1638416 | tf_op jit(solution)/shard_map/all_gather | solution.py:71
  56.8 1.8 fusion.1
  58.7 5.1 %fusion.10 = f32[3,256,256]{1,2,0:T(8,128)S(1)} fusion(bf16[3,3200,256]{2,1,0:T(8,128)(2,1)} %param.16, bf16[1,256,3200]{2,1,0:T(8,128)(2,1)} %all-gather.2.cloned.1.call-done, f32[3200]{0:T(1024)} %param.15, f32[256]{0:T(256)S(1)} %add_rsqrt_fusion.2), kind=kOutput, calls=%fused_computation.13 | convolution fusion | flops 1261568000 | bytes 7353856 | tf_op jit(solution)/shard_map/td,ide->ite/dot_general | solution.py:80
  63.8 0.1 multiply_reduce_fusion.2
  63.8 0.1 copy.51
  64.0 0.1 copy.50
  64.1 19.3 %all-reduce = (f32[256]{0:T(256)S(1)}, f32[256]{0:T(256)S(1)}) all-reduce(f32[256]{0:T(256)S(1)} %get-tuple-element.16, f32[256]{0:T(256)S(1)} %get-tuple-element.15), channel_id=1, replica_groups=mesh['req'=4,'tp'=8] {'tp'}, use_global_device_ids=true, to_apply=%region_6.7 | all-reduce | flops 512 | bytes 4096 | tf_op jit(solution)/shard_map/psum | solution.py:84
  83.4 0.3 fusion.15
  83.7 0.2 fusion.81
  83.9 0.3 convolution_convert_fusion.1
  84.2 0.0 copy-done
  84.2 2.5 fusion.82
  86.6 0.0 copy-start.4
  86.7 0.0 copy-start.5
  86.7 0.0 reduce-scatter.3.cloned.1.call-update
  86.7 0.0 copy-start.1
  86.7 0.0 copy-start.2
  86.7 0.0 reduce-scatter.5.cloned.1.call-start
  86.8 1.1 constant_dynamic-slice_fusion.1
  87.9 0.1 copy.60
  88.0 72.5 %reduce-scatter.3.cloned.1.call-done = f32[256,400]{0,1:T(8,128)} async-done(((f32[256,3200]{0,1:T(8,128)}), f32[256,400]{0,1:T(8,128)}) %reduce-scatter.3.cloned.1.call-update) | async-done | bytes 409616 | tf_op jit(solution)/shard_map/reduce_scatter | solution.py:117
  160.5 0.0 copy-done.4
  160.5 0.0 copy-done.5
  160.5 1.2 fusion.21
  161.7 0.2 copy.53
  161.9 0.3 reshape.182
  162.3 0.3 bitcast_reduce_fusion
  162.5 0.1 reduce_sum.74
  162.6 19.4 %psum.30 = f32[64]{0:T(128)S(1)} all-reduce(f32[64]{0:T(128)S(1)} %reduce_sum.74), channel_id=1, replica_groups=mesh['req'=4,'tp'=8] {'tp'}, use_global_device_ids=true, to_apply=%region_11.12 | all-reduce | flops 64 | bytes 512 | tf_op jit(solution)/shard_map/psum | solution.py:124
  182.1 0.1 sub.35
  182.1 0.5 multiply_reduce_fusion
  182.6 0.1 reduce_sum.76
  182.7 17.1 %psum.31 = f32[64]{0:T(128)S(1)} all-reduce(f32[64]{0:T(128)S(1)} %reduce_sum.76), channel_id=1, replica_groups=mesh['req'=4,'tp'=8] {'tp'}, use_global_device_ids=true, to_apply=%region_13.14 | all-reduce | flops 64 | bytes 512 | tf_op jit(solution)/shard_map/psum | solution.py:126
  199.9 0.1 copy.54
  200.0 0.0 copy-done.1
  200.0 0.0 copy-done.2
  200.0 0.0 copy-start.3
  200.0 0.0 copy-start.6
  200.0 6.7 %convolution_bitcast_fusion = f32[64,3072]{1,0:T(8,128)} fusion(bf16[4,400,3072]{2,1,0:T(8,128)(2,1)} %param.23, f32[64,4,400]{2,0,1:T(8,128)S(1)} %bitcast.63, f32[4,400]{1,0:T(4,128)S(1)} %copy-done.1, f32[4,400]{1,0:T(4,128)S(1)} %copy-done.2, f32[64]{0:T(128)S(1)} %add_rsqrt_fusion.3, f32[64]{0:T(128)S(1)} %broadcast_multiply_fusion), kind=kOutput, calls=%fused_computation.3 | convolution fusion | flops 629657600 | bytes 11039744 | tf_op jit(solution)/shard_map/dot_general | solution.py:135
  206.7 0.0 reduce-scatter.5.cloned.1.call-update
  206.7 0.5 broadcast.135
  207.2 0.0 copy-done.3
  207.2 0.7 reduce.7
  207.9 0.7 fusion.47
  208.6 0.2 reduce_window_sum.11
  208.7 0.1 reshape_reshape_squeeze.3
  208.9 0.1 copy.55
  209.0 0.1 reshape.175
  209.1 0.1 fusion.48
  209.2 58.7 %reduce-scatter.5.cloned.1.call-done = f32[8,3072]{1,0:T(8,128)} async-done(((f32[64,3072]{1,0:T(8,128)}), f32[8,3072]{1,0:T(8,128)}) %reduce-scatter.5.cloned.1.call-update) | async-done | bytes 98320 | tf_op jit(solution)/shard_map/reduce_scatter | solution.py:134
  267.9 0.0 copy-done.6
  267.9 1.2 convolution_convert_fusion
  269.2 0.1 copy.56
  269.2 6.8 %all_to_all.5 = bf16[4,3,3072]{2,1,0:T(4,128)(2,1)S(1)} all-to-all(bf16[4,3,3072]{2,1,0:T(4,128)(2,1)S(1)} %copy.56), channel_id=1, replica_groups=mesh['req'=4,'tp'=8] {'req'}, dimensions={0} | all-to-all | bytes 147456 | tf_op jit(solution)/shard_map/all_to_all | solution.py:157
  276.1 0.7 copy.57
  (10 shorter events, 0.1 us)
Async XLA Ops:
  6.5 77.6 %copy-start = (bf16[256,3200]{1,0:T(8,128)(2,1)S(1)}, bf16[256,3200]{1,0:T(8,128)(2,1)}, u32[]{:S(2)}) copy-start(bf16[256,3200]{1,0:T(8,128)(2,1)} %param.18) | copy-start | bytes 4915204
  6.5 50.3 %all-gather.2.cloned.1.call-start = ((), (), s32[]{:S(2)}) async-start(), calls=%async_computation.3 | async-start | bytes 1843200 | tf_op jit(solution)/shard_map/all_gather | solution.py:71
  7.3 153.3 %reduce-scatter.3.cloned.1.call-start = ((), (), s32[]{:S(2)}) async-start(), calls=%async_computation.4 | async-start | bytes 3686400 | tf_op jit(solution)/shard_map/reduce_scatter | solution.py:117
  86.6 73.9 %copy-start.4 = (f32[400]{0:T(512)S(1)}, f32[400]{0:T(512)}, u32[]{:S(2)}) copy-start(f32[400]{0:T(512)} %param.19) | copy-start | bytes 4804
  86.7 73.9 %copy-start.5 = (f32[400]{0:T(512)S(1)}, f32[400]{0:T(512)}, u32[]{:S(2)}) copy-start(f32[400]{0:T(512)} %param.20) | copy-start | bytes 4804
  86.7 113.3 %copy-start.1 = (f32[4,400]{1,0:T(4,128)S(1)}, f32[4,400]{1,0:T(4,128)}, u32[]{:S(2)}) copy-start(f32[4,400]{1,0:T(4,128)} %param.22) | copy-start | bytes 19204
  86.7 113.3 %copy-start.2 = (f32[4,400]{1,0:T(4,128)S(1)}, f32[4,400]{1,0:T(4,128)}, u32[]{:S(2)}) copy-start(f32[4,400]{1,0:T(4,128)} %param.21) | copy-start | bytes 19204
  86.7 181.2 %reduce-scatter.5.cloned.1.call-start = ((), (), s32[]{:S(2)}) async-start(), calls=%async_computation.5 | async-start | bytes 884736 | tf_op jit(solution)/shard_map/reduce_scatter | solution.py:134
  200.0 7.2 %copy-start.3 = (s32[1,256]{1,0:T(1,128)S(1)}, s32[1,256]{1,0:T(1,128)}, u32[]{:S(2)}) copy-start(s32[1,256]{1,0:T(1,128)} %param.14) | copy-start | bytes 3076
  200.0 67.9 %copy-start.6 = (f32[3072]{0:T(1024)S(1)}, f32[3072]{0:T(1024)}, u32[]{:S(2)}) copy-start(f32[3072]{0:T(1024)} %param.24) | copy-start | bytes 36868
Sparse Core Ops, SparseCore 0:
  9.5 47.2 all-gather.1
  86.8 73.6 reduce-scatter.2
  206.8 61.0 reduce-scatter.4
where the time goes:
time: 284 us; the launch traced here: 283 us
  waiting for transfers between devices  180 us (63%)
  blocking collectives  62.7 us (22%)
  matrix products  16.1 us (6%)
  between operations  13.3 us (5%)
  other arithmetic  5.86 us (2%)
  local copies, waits for them, and re-layouts  5.45 us (2%)
    reduce_scatter x1, waiting for transfers between devices, per_device(): lax.psum_scatter(head_part, 'tp', scatter_dimension=1, tiled=True)  72.5 us
    reduce_scatter x1, waiting for transfers between devices, per_device(): lax.psum_scatter(jnp.dot(flat_rows, flat_weight, preferred_element_type=j...  58.7 us
    all_gather x1, waiting for transfers between devices, per_device(): gathered = lax.all_gather(tokens, 'tp', axis=1, tiled=True)[0]  47.9 us
    psum x1, blocking collectives, per_device(): row_mean = lax.psum(jnp.sum(merged, axis=(1, 2)), 'tp') / feature_total  19.4 us
    psum x1, blocking collectives, per_device(): lax.psum((jnp.sum(q_part * q_part, axis=-1), jnp.sum(k_part * k_part, axi...  19.3 us
    psum x1, blocking collectives, per_device(): lax.psum(jnp.sum(centered * centered, axis=(1, 2)), 'tp') / feature_total  17.1 us
    all_to_all x1, blocking collectives, per_device(): lax.all_to_all(outgoing, 'req', split_axis=0, concat_axis=0, tiled=True)  6.83 us
    dot_general x1, matrix products, per_device(): jnp.dot(flat_rows, flat_weight, preferred_element_type=jnp.float32)  6.67 us
  transfers between devices with their start and end apart: 3, of which 3 were waited for; matrix products, arithmetic and copies ran while one was open for 2% of the time, Pallas kernels for 0%

commit v1 on v0

v1 whole, which is shorter than its diff:
```python
import functools

import jax
import jax.numpy as jnp
from jax import lax
from jax.experimental import pallas as pl
from jax.experimental.pallas import tpu as pltpu
from jax.sharding import PartitionSpec as P

HD = 128
PW = 32
EPS_RMS = 1e-06
EPS_LN = 1e-05
MESH = pl.DeviceIdType.MESH
F32 = jnp.float32
BF16 = jnp.bfloat16


def dot_nt(left, right):
    return lax.dot_general(left, right, (((1,), (1,)), ((), ())), preferred_element_type=F32)


def iota(shape, axis):
    return lax.broadcasted_iota(jnp.int32, shape, axis)


def lanes_to_column(row, count):
    return jnp.transpose(jnp.broadcast_to(row, (128, count)))


def columns_to_lanes(first, second, rows):
    lane = iota((rows, 128), 1)
    both = jnp.where(lane == 0, first, jnp.where(lane == 1, second, 0.0))
    if rows < 128:
        both = jnp.concatenate([both, jnp.zeros((128 - rows, 128), F32)], axis=0)
    return jnp.transpose(both)[:8]


def rows_to_columns(first, second, count):
    row = iota((128, count), 0)
    return jnp.transpose(jnp.where(row == 0, first, jnp.where(row == 1, second, 0.0)))


def body(
    dims,
    tok, segs, gain, qk_gain, cols, ln_w, ln_b, bm, own_ref, wqkv_h, wproj_h, wm_h,
    out,
    wqkv, wproj, wm, gathered, normed, qkv, attended,
    sb1, rb1, sb2, rb2, acc, sumbox, sumsend, statbox, statsend,
    normal, sb3, rb3, live, ob, rbo,
    wsem, ag1_s, ag2_s, ag_r, sum_s, sum_r, rs1_s, rs1_r, rs2_s, rs2_r,
    st_s, st_r, m_s, m_r, o_s, o_r,
):
    A, B, T, R, G, E, EP, S, D, M, PF, CH = dims
    me = lax.axis_index("tp")
    grp = lax.axis_index("req")
    a, b = me // B, lax.rem(me, B)
    F = wqkv.shape[2]
    MD = M // T
    W = PF // CH // 2

    wcopies = [
        pltpu.make_async_copy(wqkv_h, wqkv, wsem.at[0]),
        pltpu.make_async_copy(wproj_h, wproj, wsem.at[1]),
        pltpu.make_async_copy(wm_h, wm, wsem.at[2]),
    ]
    for copy in wcopies:
        copy.start()

    barrier = pltpu.get_barrier_semaphore()
    for i in range(1, T):
        pl.semaphore_signal(barrier, inc=1, device_id={"tp": lax.rem(me + i, T)}, device_id_type=MESH)
    for i in range(1, G):
        pl.semaphore_signal(barrier, inc=1, device_id={"req": lax.rem(grp + i, G)}, device_id_type=MESH)
    pl.semaphore_wait(barrier, T - 1 + G - 1)

    def to_tp(src, dst, s, r, peer):
        return pltpu.make_async_remote_copy(
            src_ref=src, dst_ref=dst, send_sem=s, recv_sem=r,
            device_id={"tp": peer}, device_id_type=MESH,
        )

    sends = []

    def send(copy):
        copy.start()
        sends.append(copy)

    for i in range(1, A):
        send(to_tp(tok, gathered.at[me], ag1_s.at[i - 1], ag_r.at[me], lax.rem(a + i, A) * B + b))
    for j in range(1, B):
        send(to_tp(tok, gathered.at[me], ag2_s.at[j - 1], ag_r.at[me], a * B + lax.rem(b + j, B)))
    gathered[me] = tok[...]

    def arrived(slot):
        to_tp(gathered.at[slot], gathered.at[slot], ag1_s.at[0], ag_r.at[slot], me).wait_recv()

    def normalise(slot):
        x = gathered[slot].astype(F32)
        scale = lax.rsqrt(jnp.mean(x * x, axis=-1, keepdims=True) + EPS_RMS)
        normed[slot] = (x * scale * gain[...]).astype(BF16)

    def project(slots):
        rows = jnp.concatenate([normed[s] for s in slots], axis=0)
        for i in range(3):
            part = jnp.dot(rows, wqkv[i], preferred_element_type=F32)
            for n, s in enumerate(slots):
                qkv[i, s] = part[n * R:(n + 1) * R]

    seg_row = segs[...].astype(F32)
    seg_col = lanes_to_column(seg_row, S)
    token = iota((M, S), 1)
    merged_id = iota((M, S), 0)
    half = PW // 2
    base = 2 * PW * (merged_id // half) + 2 * lax.rem(merged_id, half)
    live[...] = jnp.dot(
        (token == base).astype(BF16), (seg_col >= 0).astype(BF16), preferred_element_type=F32
    )

    normalise(me)
    for i in range(1, A):
        slot = lax.rem(a + A - i, A) * B + b
        arrived(slot)
        for j in range(1, B):
            send(to_tp(
                gathered.at[slot], gathered.at[slot], ag2_s.at[i * (B - 1) + j - 1],
                ag_r.at[slot], a * B + lax.rem(b + j, B),
            ))
        normalise(slot)
    wcopies[0].wait()
    project([lax.rem(a + A - i, A) * B + b for i in range(A)])
    for j in range(1, B):
        slots = [lax.rem(a + A - i, A) * B + lax.rem(b + B - j, B) for i in range(A)]
        for slot in slots:
            arrived(slot)
            normalise(slot)
        project(slots)

    q_part = qkv[0].reshape(S, F)
    k_part = qkv[1].reshape(S, F)
    sumsend[...] = columns_to_lanes(
        jnp.sum(q_part * q_part, axis=-1, keepdims=True),
        jnp.sum(k_part * k_part, axis=-1, keepdims=True), S,
    )
    for i in range(1, T):
        send(to_tp(sumsend, sumbox.at[me], sum_s.at[i - 1], sum_r.at[me], lax.rem(me + i, T)))
    sumbox[me] = sumsend[...]
    for i in range(1, T):
        slot = lax.rem(me + i, T)
        to_tp(sumsend, sumbox.at[slot], sum_s.at[0], sum_r.at[slot], me).wait_recv()
    total = jnp.sum(sumbox[...], axis=0)
    inner = F * T
    scales = lax.rsqrt(total / inner + EPS_RMS)
    columns = rows_to_columns(scales[0:1], scales[1:2], S)
    q_all = (qkv[0].reshape(S, F) * columns[:, 0:1] * qk_gain[0:1, :]).astype(BF16)
    k_all = (qkv[1].reshape(S, F) * columns[:, 1:2] * qk_gain[1:2, :]).astype(BF16)
    v_all = qkv[2].reshape(S, F).astype(BF16)
    same = lanes_to_column(seg_row, S)[:, 0:1] == seg_row
    for h in range(F // HD):
        lo, hi = h * HD, (h + 1) * HD
        scores = jnp.where(same, dot_nt(q_all[:, lo:hi], k_all[:, lo:hi]) * HD ** (-0.5), -jnp.inf)
        weights = jnp.exp(scores - jnp.max(scores, axis=-1, keepdims=True))
        probabilities = (weights / jnp.sum(weights, axis=-1, keepdims=True)).astype(BF16)
        attended[:, lo:hi] = jnp.dot(
            probabilities, v_all[:, lo:hi], preferred_element_type=F32
        ).astype(BF16)

    wcopies[1].wait()
    for i in list(range(1, A)) + [0]:
        for j in range(1, B):
            dest_a, dest_b = lax.rem(a + i, A), lax.rem(b + j, B)
            sb1[j - 1, i] = dot_nt(wproj[dest_a * B + dest_b], attended[...]).astype(BF16)
            send(to_tp(sb1.at[j - 1, i], rb1.at[j - 1, i], rs1_s.at[j - 1, i],
                       rs1_r.at[j - 1, i], a * B + dest_b))
    for i in list(range(1, A)) + [0]:
        dest_a = lax.rem(a + i, A)
        part = dot_nt(wproj[dest_a * B + b], attended[...])
        for j in range(1, B):
            to_tp(sb1.at[j - 1, i], rb1.at[j - 1, i], rs1_s.at[j - 1, i],
                  rs1_r.at[j - 1, i], me).wait_recv()
            part = part + rb1[j - 1, i].astype(F32)
        if i:
            sb2[i - 1] = part.astype(BF16)
            send(to_tp(sb2.at[i - 1], rb2.at[i - 1], rs2_s.at[i - 1], rs2_r.at[i - 1],
                       dest_a * B + b))
        else:
            acc[...] = part
    KC = D // 5
    own = jnp.zeros((EP, S), F32)
    for c in range(5):
        pick = (iota((EP, KC), 1) + c * KC == iota((EP, KC), 0) + me * E).astype(BF16)
        own = own + dot_nt(pick, gathered[:, :, c * KC:(c + 1) * KC].reshape(S, KC))
    for i in range(1, A):
        to_tp(sb2.at[i - 1], rb2.at[i - 1], rs2_s.at[i - 1], rs2_r.at[i - 1], me).wait_recv()
    attn = acc[...]
    for i in range(1, A):
        attn = attn + rb2[i - 1].astype(F32)
    stream = (own + cols[:, 1:2] * (attn + cols[:, 0:1])).astype(BF16)

    merged = []
    for off in (0, 1, PW, PW + 1):
        merged.append(dot_nt((token == base + off).astype(BF16), stream)[:, :E])
    local = sum(jnp.sum(m, axis=-1, keepdims=True) for m in merged)
    local_mean = local / (4 * E)
    spread = sum(jnp.sum((m - local_mean) * (m - local_mean), axis=-1, keepdims=True) for m in merged)
    statsend[...] = columns_to_lanes(local, spread, M)
    for i in range(1, T):
        send(to_tp(statsend, statbox.at[me], st_s.at[i - 1], st_r.at[me], lax.rem(me + i, T)))
    statbox[me] = statsend[...]
    for i in range(1, T):
        slot = lax.rem(me + i, T)
        to_tp(statsend, statbox.at[slot], st_s.at[0], st_r.at[slot], me).wait_recv()
    stats = [statbox[t] for t in range(T)]
    mean_row = sum(s[0:1] for s in stats) / (4 * D)
    square_row = sum(s[1:2] for s in stats) + (4 * E) * sum(
        (s[0:1] / (4 * E) - mean_row) * (s[0:1] / (4 * E) - mean_row) for s in stats
    )
    stat_cols = rows_to_columns(mean_row, lax.rsqrt(square_row / (4 * D) + EPS_LN), 128)[:M]
    row_mean, row_scale = stat_cols[:, 0:1], stat_cols[:, 1:2]
    for n in range(4):
        normal[n] = (
            (merged[n] - row_mean) * row_scale * ln_w[n:n + 1, :] + ln_b[n:n + 1, :]
        ).astype(BF16)

    wcopies[2].wait()
    for c in range(CH):
        lo = 2 * W * c
        part = sum(
            jnp.dot(normal[n], wm[n, :, lo:lo + 2 * W], preferred_element_type=F32)
            for n in range(4)
        )
        for k in range(T):
            rows = part[k * MD:(k + 1) * MD]
            sb3[c, k] = jnp.concatenate([rows[:, :W], rows[:, W:]], axis=0).astype(BF16)
        rb3[c, me] = sb3[c, me]
        for i in range(1, T):
            peer = lax.rem(me + i, T)
            send(to_tp(sb3.at[c, peer], rb3.at[c, me], m_s.at[c, i - 1], m_r.at[c, me], peer))

    ids = jnp.broadcast_to(own_ref[grp].astype(F32), (MD, 128))
    ids_row = jnp.transpose(jnp.concatenate([ids] * (128 // MD), axis=0))
    lane = iota((MD, 128), 1)
    earlier = (ids == ids_row[:MD]) & (iota((MD, 128), 0) < lax.rem(lane, MD))
    rank = jnp.sum(earlier.astype(F32), axis=0, keepdims=True)
    N = 2 * CH
    rows = iota((G * 4 * N, 128), 0)
    lane = iota((G * 4 * N, 128), 1)
    pick = (
        (ids_row[0:1] == (rows // (4 * N)).astype(F32))
        & (rank == lax.rem(rows, 4).astype(F32))
        & (lane // MD == lax.rem(rows, 4 * N) // 4)
    )
    pick = pick.astype(BF16)[:, :N * MD]
    alive = live[pl.ds(pl.multiple_of(me * MD, MD), MD), :][:, 0:1]
    pieces = []
    for c in range(CH):
        for i in range(1, T):
            slot = lax.rem(me + i, T)
            to_tp(sb3.at[c, slot], rb3.at[c, slot], m_s.at[c, 0], m_r.at[c, slot], me).wait_recv()
        total = rb3[c, 0].astype(F32)
        for k in range(1, T):
            total = total + rb3[c, k].astype(F32)
        for h in range(2):
            at = (2 * c + h) * W
            x = total[h * MD:(h + 1) * MD] + bm[:, at:at + W]
            pieces.append(0.5 * x * (1.0 + lax.erf(x * (0.5 ** 0.5))) * alive)
    stacked = jnp.concatenate(pieces, axis=0).astype(BF16)
    ob[...] = jnp.dot(pick, stacked, preferred_element_type=F32).reshape(G, 4 * N, W).astype(BF16)
    for i in range(1, G):
        peer = lax.rem(grp + i, G)
        copy = pltpu.make_async_remote_copy(
            src_ref=ob.at[peer], dst_ref=rbo.at[grp], send_sem=o_s.at[i - 1],
            recv_sem=o_r.at[grp], device_id={"req": peer}, device_id_type=MESH,
        )
        copy.start()
        sends.append(copy)
    out[grp] = ob[grp]
    for i in range(1, G):
        slot = lax.rem(grp + i, G)
        pltpu.make_async_remote_copy(
            src_ref=ob.at[slot], dst_ref=rbo.at[slot], send_sem=o_s.at[0],
            recv_sem=o_r.at[slot], device_id={"req": grp}, device_id_type=MESH,
        ).wait_recv()
        out[slot] = rbo[slot]
    for copy in sends:
        copy.wait_send()


def per_device(
    tokens, segments, norm_gain, wqkv, qk_gain, wproj, bproj, layer_scale,
    ln_weight, ln_bias, w_merge, b_merge, owners,
):
    T = lax.axis_size("tp")
    G = lax.axis_size("req")
    A = 4
    B = T // A
    R, D = tokens.shape[1:]
    S = R * T
    F = wqkv.shape[2]
    E = bproj.shape[0]
    EP = -(-E // 16) * 16
    M = S // 4
    MD = M // T
    PF = w_merge.shape[2]
    CH = 2
    W = PF // CH // 2
    capacity = (MD + G - 1) // G + 1
    wproj_t = wproj.T.reshape(T, E, F)
    cols = jnp.stack([bproj, layer_scale], axis=1)
    if EP != E:
        wproj_t = jnp.pad(wproj_t, ((0, 0), (0, EP - E), (0, 0)))
        cols = jnp.pad(cols, ((0, EP - E), (0, 0)))
    dims = (A, B, T, R, G, E, EP, S, D, M, PF, CH)
    vmem = pl.BlockSpec(memory_space=pltpu.VMEM)
    hbm = pl.BlockSpec(memory_space=pl.ANY)
    dma = pltpu.SemaphoreType.DMA
    out = pl.pallas_call(
        functools.partial(body, dims),
        out_shape=jax.ShapeDtypeStruct((G, 8 * CH, W), BF16),
        in_specs=[vmem] * 9 + [hbm] * 3,
        out_specs=vmem,
        scratch_shapes=[
            pltpu.VMEM((3, D, F), BF16),
            pltpu.VMEM((T, EP, F), BF16),
            pltpu.VMEM((4, E, PF), BF16),
            pltpu.VMEM((T, R, D), BF16),
            pltpu.VMEM((T, R, D), BF16),
            pltpu.VMEM((3, T, R, F), F32),
            pltpu.VMEM((S, F), BF16),
            pltpu.VMEM((B - 1, A, EP, S), BF16),
            pltpu.VMEM((B - 1, A, EP, S), BF16),
            pltpu.VMEM((A - 1, EP, S), BF16),
            pltpu.VMEM((A - 1, EP, S), BF16),
            pltpu.VMEM((EP, S), F32),
            pltpu.VMEM((T, 8, S), F32),
            pltpu.VMEM((8, S), F32),
            pltpu.VMEM((T, 8, 128), F32),
            pltpu.VMEM((8, 128), F32),
            pltpu.VMEM((4, M, E), BF16),
            pltpu.VMEM((CH, T, 2 * MD, W), BF16),
            pltpu.VMEM((CH, T, 2 * MD, W), BF16),
            pltpu.VMEM((M, 128), F32),
            pltpu.VMEM((G, 8 * CH, W), BF16),
            pltpu.VMEM((G, 8 * CH, W), BF16),
            dma((3,)),
            dma((A - 1,)), dma((A * (B - 1),)), dma((T,)),
            dma((T - 1,)), dma((T,)),
            dma((B - 1, A)), dma((B - 1, A)),
            dma((A - 1,)), dma((A - 1,)),
            dma((T - 1,)), dma((T,)),
            dma((CH, T - 1)), dma((CH, T)),
            dma((G - 1,)), dma((G,)),
        ],
        compiler_params=pltpu.CompilerParams(
            collective_id=0, has_side_effects=True, vmem_limit_bytes=56 * 1024 * 1024
        ),
    )(
        tokens[0], segments, norm_gain.reshape(1, D), qk_gain, cols, ln_weight, ln_bias,
        b_merge.reshape(1, PF), owners, wqkv, wproj_t, w_merge,
    )
    slots = out.reshape(G, 2 * CH, 4, W).transpose(0, 2, 1, 3).reshape(G, 4, PF)
    return slots[:, :capacity].reshape(1, G, 1, capacity, PF)


def solution(mesh):
    placed = (
        P("req", "tp", None),
        P("req", None),
        P(),
        P(None, None, "tp"),
        P(None, "tp"),
        P("tp", None),
        P("tp"),
        P("tp"),
        P(None, "tp"),
        P(None, "tp"),
        P(None, "tp", None),
        P(),
        P(None, "tp", None),
    )
    return jax.shard_map(
        per_device,
        mesh=mesh,
        in_specs=placed,
        out_specs=P("req", None, "tp", None, None),
        check_vma=False,
    )
```

time: 284 us -> 93 us (0.33)
  waiting for transfers between devices: 180 us -> 0 us
  Pallas kernels: 0 us -> 83 us
  blocking collectives: 62.7 us -> 0 us
  matrix products: 16.1 us -> 0 us
  between operations: 13.3 us -> 0.03 us
  other arithmetic: 5.86 us -> 0.71 us
  local copies, waits for them, and re-layouts: 5.45 us -> 8.9 us
    reduce_scatter x2 -> x0, waiting for transfers between devices: 131 us -> none  [the longest x1 72.5 us: per_device(): lax.psum_scatter(head_part, 'tp', scatter_dimension=1, tiled=True)]
    pallas_call x0 -> x1, Pallas kernels: none -> 83 us  [per_device(): pl.pallas_call(functools.partial(body, dims), out_shape=jax.ShapeDtypeStr...]
    psum x3 -> x0, blocking collectives: 55.8 us -> none  [the longest x1 19.4 us: per_device(): row_mean = lax.psum(jnp.sum(merged, axis=(1, 2)), 'tp') / feature_total]
    all_gather x1 -> x0, waiting for transfers between devices: 47.9 us -> none  [per_device(): gathered = lax.all_gather(tokens, 'tp', axis=1, tiled=True)[0]]
    dot_general x6 -> x0, matrix products: 16.1 us -> none  [the longest x1 6.67 us: per_device(): jnp.dot(flat_rows, flat_weight, preferred_element_type=jnp.float32)]
    all_to_all x1 -> x0, blocking collectives: 6.83 us -> none  [per_device(): lax.all_to_all(outgoing, 'req', split_axis=0, concat_axis=0, tiled=True)]
    transpose x1 -> x2, local copies, waits for them, and re-layouts: 0.12 us -> 3.73 us  [the longest x1 3.69 us: per_device(): wproj_t = wproj.T.reshape(T, E, F)]
  transfers between devices with their start and end apart: 3 -> 0, of which waited for: 3 -> 0; matrix products, arithmetic and copies ran while one was open for 2% -> 0% of each run, Pallas kernels for 0% -> 0%
where the time goes in v1:
time: 93 us; the launch traced here: 92.7 us
  Pallas kernels  83 us (89%)
  local copies, waits for them, and re-layouts  8.9 us (10%)
    pallas_call x1, Pallas kernels, per_device(): pl.pallas_call(functools.partial(body, dims), out_shape=jax.ShapeDtypeStr...  83 us
    transpose x1, local copies, waits for them, and re-layouts, per_device(): wproj_t = wproj.T.reshape(T, E, F)  3.69 us

profile of v1, /device:TPU:0, one launch (start us, length us, event | category | flops | bytes accessed | tf_op | source)
XLA Modules:
  0.0 92.7 jit_solution(1020218986471723250)
XLA Ops:
  0.0 0.7 pad_maximum_fusion
  0.7 1.3 %reshape.18.gain = f32[1,3200]{1,0:T(1,128)} reshape(f32[3200]{0:T(1024)} %param.15) | data formatting | bytes 25600 | tf_op jit(solution)/shard_map/reshape | solution.py:358
  2.0 1.4 %copy.24.own_ref = s32[4,8,1]{2,1,0:T(8,128)} copy(s32[4,8,1]{1,2,0:T(1,128)} %param.25) | data formatting | bytes 256 | tf_op args[12]
  3.4 0.8 copy.23.cols
  4.3 3.7 %copy.22 = bf16[3200,256]{1,0:T(8,128)(2,1)} copy(bf16[3200,256]{0,1:T(8,128)(2,1)} %bitcast.12) | data formatting | bytes 3276800 | tf_op jit(solution)/shard_map/transpose | solution.py:308
  7.9 83.0 %shard_map.127 = bf16[4,16,768]{2,1,0:T(8,128)(2,1)} custom-call(bf16[32,3200]{1,0:T(8,128)(2,1)} %bitcast.14, s32[1,256]{1,0:T(1,128)} %segs.1, f32[1,3200]{1,0:T(1,128)} %reshape.18.gain, f32[2,256]{1,0:T(2,128)} %qk_gain.1, f32[400,2]{1,0:T(8,128)} %copy.23.cols, f32[4,400]{1,0:T(4,128)} %ln_w.1, f32[4,400]{1,0:T(4,128)} %ln_b.1, f32[1,3072]{1,0:T(1,128)} %bitcast.15, ...), custom_call_target="tpu_custom_call" | custom-call | tf_op jit(solution)/shard_map/pallas_call | solution.py:317
  91.0 0.9 reshape.21
  92.0 0.7 slice_bitcast_fusion
  (2 shorter events, 0.1 us)

commit v2 on v1

--- a/solution.py
+++ b/solution.py
@@ -43,11 +43,11 @@
 
 def body(
     dims,
-    tok, segs, gain, qk_gain, cols, ln_w, ln_b, bm, own_ref, wqkv_h, wproj_h, wm_h,
+    tok, segs, gain, qk_gain, bias, lscale, ln_w, ln_b, bm, own_ref, wqkv_h, wproj_h, wm_h,
     out,
-    wqkv, wproj, wm, gathered, normed, qkv, attended,
+    wqkv, wproj_v, wm, turned, wproj, cols, gathered, normed, qkv, attended,
     sb1, rb1, sb2, rb2, acc, sumbox, sumsend, statbox, statsend,
-    normal, sb3, rb3, live, ob, rbo,
+    normal, sb3, rb3, live, ob, rbo, raw,
     wsem, ag1_s, ag2_s, ag_r, sum_s, sum_r, rs1_s, rs1_r, rs2_s, rs2_r,
     st_s, st_r, m_s, m_r, o_s, o_r,
 ):
@@ -61,7 +61,7 @@
 
     wcopies = [
         pltpu.make_async_copy(wqkv_h, wqkv, wsem.at[0]),
-        pltpu.make_async_copy(wproj_h, wproj, wsem.at[1]),
+        pltpu.make_async_copy(wproj_h, wproj_v, wsem.at[1]),
         pltpu.make_async_copy(wm_h, wm, wsem.at[2]),
     ]
     for copy in wcopies:
@@ -86,19 +86,24 @@
         copy.start()
         sends.append(copy)
 
-    for i in range(1, A):
-        send(to_tp(tok, gathered.at[me], ag1_s.at[i - 1], ag_r.at[me], lax.rem(a + i, A) * B + b))
-    for j in range(1, B):
-        send(to_tp(tok, gathered.at[me], ag2_s.at[j - 1], ag_r.at[me], a * B + lax.rem(b + j, B)))
+    C = gathered.shape[1]
+    for c in range(C):
+        for j in range(1, B):
+            send(to_tp(tok.at[c], gathered.at[me, c], ag2_s.at[c, j - 1], ag_r.at[me, c],
+                       a * B + lax.rem(b + j, B)))
+        for i in range(1, A):
+            send(to_tp(tok.at[c], gathered.at[me, c], ag1_s.at[c, i - 1], ag_r.at[me, c],
+                       lax.rem(a + i, A) * B + b))
     gathered[me] = tok[...]
 
-    def arrived(slot):
-        to_tp(gathered.at[slot], gathered.at[slot], ag1_s.at[0], ag_r.at[slot], me).wait_recv()
+    def arrived(slot, c):
+        to_tp(gathered.at[slot, c], gathered.at[slot, c], ag1_s.at[0, 0], ag_r.at[slot, c],
+              me).wait_recv()
 
     def normalise(slot):
-        x = gathered[slot].astype(F32)
+        x = gathered[slot].reshape(R, D).astype(F32)
         scale = lax.rsqrt(jnp.mean(x * x, axis=-1, keepdims=True) + EPS_RMS)
-        normed[slot] = (x * scale * gain[...]).astype(BF16)
+        normed[slot] = (x * scale * gain[...].reshape(1, D)).astype(BF16)
 
     def project(slots):
         rows = jnp.concatenate([normed[s] for s in slots], axis=0)
@@ -117,22 +122,42 @@
         (token == base).astype(BF16), (seg_col >= 0).astype(BF16), preferred_element_type=F32
     )
 
-    normalise(me)
-    for i in range(1, A):
-        slot = lax.rem(a + A - i, A) * B + b
-        arrived(slot)
-        for j in range(1, B):
-            send(to_tp(
-                gathered.at[slot], gathered.at[slot], ag2_s.at[i * (B - 1) + j - 1],
-                ag_r.at[slot], a * B + lax.rem(b + j, B),
-            ))
+    first = [lax.rem(a + A - i, A) * B + b for i in range(A)]
+    for c in range(C):
+        for i in range(1, A):
+            slot = first[i]
+            arrived(slot, c)
+            for j in range(1, B):
+                send(to_tp(
+                    gathered.at[slot, c], gathered.at[slot, c],
+                    ag2_s.at[c, i * (B - 1) + j - 1], ag_r.at[slot, c], a * B + lax.rem(b + j, B),
+                ))
+    for slot in first:
         normalise(slot)
     wcopies[0].wait()
-    project([lax.rem(a + A - i, A) * B + b for i in range(A)])
+    project(first)
+    wcopies[1].wait()
+    KC = D // 5
+    for c in range(5):
+        turned[c * KC:(c + 1) * KC, :] = jnp.transpose(
+            wproj_v[:, c * KC:(c + 1) * KC].astype(F32)
+        )
+    for k in range(T):
+        block = turned[k * E:(k + 1) * E, :]
+        if EP != E:
+            block = jnp.concatenate([block, jnp.zeros((EP - E, F), F32)], axis=0)
+        wproj[k] = block.astype(BF16)
+    row = iota((8, E), 0)
+    two = jnp.where(row == 0, bias[...].reshape(1, E), jnp.where(row == 1, lscale[...].reshape(1, E), 0.0))
+    cols[...] = lax.dot_general(
+        (iota((EP, E), 0) == iota((EP, E), 1)).astype(F32), two, (((1,), (1,)), ((), ())),
+        precision=lax.Precision.HIGHEST, preferred_element_type=F32,
+    )
     for j in range(1, B):
         slots = [lax.rem(a + A - i, A) * B + lax.rem(b + B - j, B) for i in range(A)]
         for slot in slots:
-            arrived(slot)
+            for c in range(C):
+                arrived(slot, c)
             normalise(slot)
         project(slots)
 
@@ -145,27 +170,28 @@
     for i in range(1, T):
         send(to_tp(sumsend, sumbox.at[me], sum_s.at[i - 1], sum_r.at[me], lax.rem(me + i, T)))
     sumbox[me] = sumsend[...]
+    q_all = (q_part * qk_gain[0:1, :]).astype(BF16)
+    k_all = (k_part * qk_gain[1:2, :]).astype(BF16)
+    v_all = qkv[2].reshape(S, F).astype(BF16)
+    same = lanes_to_column(seg_row, S)[:, 0:1] == seg_row
+    for h in range(F // HD):
+        raw[h] = dot_nt(q_all[:, h * HD:(h + 1) * HD], k_all[:, h * HD:(h + 1) * HD])
     for i in range(1, T):
         slot = lax.rem(me + i, T)
         to_tp(sumsend, sumbox.at[slot], sum_s.at[0], sum_r.at[slot], me).wait_recv()
     total = jnp.sum(sumbox[...], axis=0)
     inner = F * T
     scales = lax.rsqrt(total / inner + EPS_RMS)
-    columns = rows_to_columns(scales[0:1], scales[1:2], S)
-    q_all = (qkv[0].reshape(S, F) * columns[:, 0:1] * qk_gain[0:1, :]).astype(BF16)
-    k_all = (qkv[1].reshape(S, F) * columns[:, 1:2] * qk_gain[1:2, :]).astype(BF16)
-    v_all = qkv[2].reshape(S, F).astype(BF16)
-    same = lanes_to_column(seg_row, S)[:, 0:1] == seg_row
+    query_scale = lanes_to_column(scales[0:1], S)[:, 0:1] * HD ** (-0.5)
     for h in range(F // HD):
         lo, hi = h * HD, (h + 1) * HD
-        scores = jnp.where(same, dot_nt(q_all[:, lo:hi], k_all[:, lo:hi]) * HD ** (-0.5), -jnp.inf)
+        scores = jnp.where(same, raw[h] * query_scale * scales[1:2], -jnp.inf)
         weights = jnp.exp(scores - jnp.max(scores, axis=-1, keepdims=True))
         probabilities = (weights / jnp.sum(weights, axis=-1, keepdims=True)).astype(BF16)
         attended[:, lo:hi] = jnp.dot(
             probabilities, v_all[:, lo:hi], preferred_element_type=F32
         ).astype(BF16)
 
-    wcopies[1].wait()
     for i in list(range(1, A)) + [0]:
         for j in range(1, B):
             dest_a, dest_b = lax.rem(a + i, A), lax.rem(b + j, B)
@@ -185,11 +211,10 @@
                        dest_a * B + b))
         else:
             acc[...] = part
-    KC = D // 5
     own = jnp.zeros((EP, S), F32)
     for c in range(5):
         pick = (iota((EP, KC), 1) + c * KC == iota((EP, KC), 0) + me * E).astype(BF16)
-        own = own + dot_nt(pick, gathered[:, :, c * KC:(c + 1) * KC].reshape(S, KC))
+        own = own + dot_nt(pick, gathered[:, :, :, c * KC:(c + 1) * KC].reshape(S, KC))
     for i in range(1, A):
         to_tp(sb2.at[i - 1], rb2.at[i - 1], rs2_s.at[i - 1], rs2_r.at[i - 1], me).wait_recv()
     attn = acc[...]
@@ -237,8 +262,12 @@
             peer = lax.rem(me + i, T)
             send(to_tp(sb3.at[c, peer], rb3.at[c, me], m_s.at[c, i - 1], m_r.at[c, me], peer))
 
-    ids = jnp.broadcast_to(own_ref[grp].astype(F32), (MD, 128))
-    ids_row = jnp.transpose(jnp.concatenate([ids] * (128 // MD), axis=0))
+    spot = (lax.rem(iota((MD, 128), 1), MD) == iota((MD, 128), 0)).astype(F32)
+    ids_row = jnp.dot(
+        jnp.broadcast_to(own_ref[pl.ds(grp, 1), :].astype(F32), (128, MD)), spot,
+        preferred_element_type=F32,
+    )
+    ids = jnp.transpose(ids_row)[:MD]
     lane = iota((MD, 128), 1)
     earlier = (ids == ids_row[:MD]) & (iota((MD, 128), 0) < lax.rem(lane, MD))
     rank = jnp.sum(earlier.astype(F32), axis=0, keepdims=True)
@@ -262,7 +291,7 @@
             total = total + rb3[c, k].astype(F32)
         for h in range(2):
             at = (2 * c + h) * W
-            x = total[h * MD:(h + 1) * MD] + bm[:, at:at + W]
+            x = total[h * MD:(h + 1) * MD] + bm[at:at + W].reshape(1, W)
             pieces.append(0.5 * x * (1.0 + lax.erf(x * (0.5 ** 0.5))) * alive)
     stacked = jnp.concatenate(pieces, axis=0).astype(BF16)
     ob[...] = jnp.dot(pick, stacked, preferred_element_type=F32).reshape(G, 4 * N, W).astype(BF16)
@@ -305,11 +334,7 @@
     CH = 2
     W = PF // CH // 2
     capacity = (MD + G - 1) // G + 1
-    wproj_t = wproj.T.reshape(T, E, F)
-    cols = jnp.stack([bproj, layer_scale], axis=1)
-    if EP != E:
-        wproj_t = jnp.pad(wproj_t, ((0, 0), (0, EP - E), (0, 0)))
-        cols = jnp.pad(cols, ((0, EP - E), (0, 0)))
+    C = 2
     dims = (A, B, T, R, G, E, EP, S, D, M, PF, CH)
     vmem = pl.BlockSpec(memory_space=pltpu.VMEM)
     hbm = pl.BlockSpec(memory_space=pl.ANY)
@@ -317,13 +342,16 @@
     out = pl.pallas_call(
         functools.partial(body, dims),
         out_shape=jax.ShapeDtypeStruct((G, 8 * CH, W), BF16),
-        in_specs=[vmem] * 9 + [hbm] * 3,
+        in_specs=[vmem] * 10 + [hbm] * 3,
         out_specs=vmem,
         scratch_shapes=[
             pltpu.VMEM((3, D, F), BF16),
+            pltpu.VMEM((F, D), BF16),
+            pltpu.VMEM((4, E, PF), BF16),
+            pltpu.VMEM((D, F), F32),
             pltpu.VMEM((T, EP, F), BF16),
-            pltpu.VMEM((4, E, PF), BF16),
-            pltpu.VMEM((T, R, D), BF16),
+            pltpu.VMEM((EP, 8), F32),
+            pltpu.VMEM((T, C, R // C, D), BF16),
             pltpu.VMEM((T, R, D), BF16),
             pltpu.VMEM((3, T, R, F), F32),
             pltpu.VMEM((S, F), BF16),
@@ -342,8 +370,9 @@
             pltpu.VMEM((M, 128), F32),
             pltpu.VMEM((G, 8 * CH, W), BF16),
             pltpu.VMEM((G, 8 * CH, W), BF16),
+            pltpu.VMEM((F // HD, S, S), F32),
             dma((3,)),
-            dma((A - 1,)), dma((A * (B - 1),)), dma((T,)),
+            dma((C, A - 1)), dma((C, A * (B - 1))), dma((T, C)),
             dma((T - 1,)), dma((T,)),
             dma((B - 1, A)), dma((B - 1, A)),
             dma((A - 1,)), dma((A - 1,)),
@@ -355,8 +384,8 @@
             collective_id=0, has_side_effects=True, vmem_limit_bytes=56 * 1024 * 1024
         ),
     )(
-        tokens[0], segments, norm_gain.reshape(1, D), qk_gain, cols, ln_weight, ln_bias,
-        b_merge.reshape(1, PF), owners, wqkv, wproj_t, w_merge,
+        tokens.reshape(C, R // C, D), segments, norm_gain, qk_gain, bproj, layer_scale,
+        ln_weight, ln_bias, b_merge, owners[:, :, 0], wqkv, wproj, w_merge,
     )
     slots = out.reshape(G, 2 * CH, 4, W).transpose(0, 2, 1, 3).reshape(G, 4, PF)
     return slots[:, :capacity].reshape(1, G, 1, capacity, PF)

time: 93 us -> 81 us (0.87)
  local copies, waits for them, and re-layouts: 8.9 us -> 1.66 us
  Pallas kernels: 83 us -> 79.1 us
    pallas_call x1, Pallas kernels: 83 us -> 79.1 us  [per_device(): pl.pallas_call(functools.partial(body, dims), out_shape=jax.ShapeDtypeStr...]
    transpose x1 -> x0, local copies, waits for them, and re-layouts: 3.69 us -> none  [per_device(): wproj_t = wproj.T.reshape(T, E, F)]
    unnamed x1 -> x0, local copies, waits for them, and re-layouts: 1.38 us -> none
    reshape x1 -> x0, local copies, waits for them, and re-layouts: 1.33 us -> none  [per_device(): norm_gain.reshape(1, D)]
where the time goes in v2:
time: 81 us; the launch traced here: 80.8 us
  Pallas kernels  79.1 us (98%)
  local copies, waits for them, and re-layouts  1.66 us (2%)
    pallas_call x1, Pallas kernels, per_device(): pl.pallas_call(functools.partial(body, dims), out_shape=jax.ShapeDtypeStr...  79.1 us

profile of v2, /device:TPU:0, one launch (start us, length us, event | category | flops | bytes accessed | tf_op | source)
XLA Modules:
  0.0 80.8 jit_solution(6159529331816256300)
XLA Ops:
  0.0 79.1 %shard_map.127 = bf16[4,16,768]{2,1,0:T(8,128)(2,1)} custom-call(bf16[2,16,3200]{2,1,0:T(8,128)(2,1)} %bitcast.8, s32[1,256]{1,0:T(1,128)} %segs.1, f32[3200]{0:T(1024)} %gain.1, f32[2,256]{1,0:T(2,128)} %qk_gain.1, f32[400]{0:T(512)} %bias.1, f32[400]{0:T(512)} %lscale.1, f32[4,400]{1,0:T(4,128)} %ln_w.1, f32[4,400]{1,0:T(4,128)} %ln_b.1, f32[3072]{0:T(1024)} %bm.1, ...), custom_call_target="tpu_custom_call" | custom-call | tf_op jit(solution)/shard_map/pallas_call | solution.py:342
  79.1 0.9 %reshape.13 = bf16[4,4,4,768]{3,2,1,0:T(4,128)(2,1)S(1)} reshape(bf16[4,16,768]{2,1,0:T(8,128)(2,1)} %shard_map.127) | data formatting | bytes 196608 | tf_op jit(solution)/shard_map/reshape | solution.py:390
  80.2 0.7 slice_bitcast_fusion
  (2 shorter events, 0.1 us)

commit v3 on v2

--- a/solution.py
+++ b/solution.py
@@ -87,13 +87,14 @@
         sends.append(copy)
 
     C = gathered.shape[1]
+    partners = [a, a + 1 - 2 * lax.rem(a, 2), lax.rem(a + 2, A), A - 1 - a]
     for c in range(C):
         for j in range(1, B):
             send(to_tp(tok.at[c], gathered.at[me, c], ag2_s.at[c, j - 1], ag_r.at[me, c],
                        a * B + lax.rem(b + j, B)))
         for i in range(1, A):
             send(to_tp(tok.at[c], gathered.at[me, c], ag1_s.at[c, i - 1], ag_r.at[me, c],
-                       lax.rem(a + i, A) * B + b))
+                       partners[i] * B + b))
     gathered[me] = tok[...]
 
     def arrived(slot, c):
@@ -105,9 +106,9 @@
         scale = lax.rsqrt(jnp.mean(x * x, axis=-1, keepdims=True) + EPS_RMS)
         normed[slot] = (x * scale * gain[...].reshape(1, D)).astype(BF16)
 
-    def project(slots):
+    def project(slots, which=(0, 1, 2)):
         rows = jnp.concatenate([normed[s] for s in slots], axis=0)
-        for i in range(3):
+        for i in which:
             part = jnp.dot(rows, wqkv[i], preferred_element_type=F32)
             for n, s in enumerate(slots):
                 qkv[i, s] = part[n * R:(n + 1) * R]
@@ -122,7 +123,7 @@
         (token == base).astype(BF16), (seg_col >= 0).astype(BF16), preferred_element_type=F32
     )
 
-    first = [lax.rem(a + A - i, A) * B + b for i in range(A)]
+    first = [p * B + b for p in partners]
     for c in range(C):
         for i in range(1, A):
             slot = first[i]
@@ -154,12 +155,12 @@
         precision=lax.Precision.HIGHEST, preferred_element_type=F32,
     )
     for j in range(1, B):
-        slots = [lax.rem(a + A - i, A) * B + lax.rem(b + B - j, B) for i in range(A)]
+        slots = [p * B + lax.rem(b + B - j, B) for p in partners]
         for slot in slots:
             for c in range(C):
                 arrived(slot, c)
             normalise(slot)
-        project(slots)
+        project(slots, (0, 1) if j == B - 1 else (0, 1, 2))
 
     q_part = qkv[0].reshape(S, F)
     k_part = qkv[1].reshape(S, F)
@@ -170,6 +171,7 @@
     for i in range(1, T):
         send(to_tp(sumsend, sumbox.at[me], sum_s.at[i - 1], sum_r.at[me], lax.rem(me + i, T)))
     sumbox[me] = sumsend[...]
+    project(slots, (2,))
     q_all = (q_part * qk_gain[0:1, :]).astype(BF16)
     k_all = (k_part * qk_gain[1:2, :]).astype(BF16)
     v_all = qkv[2].reshape(S, F).astype(BF16)
@@ -303,14 +305,19 @@
         )
         copy.start()
         sends.append(copy)
-    out[grp] = ob[grp]
+    rbo[grp] = ob[grp]
     for i in range(1, G):
         slot = lax.rem(grp + i, G)
         pltpu.make_async_remote_copy(
             src_ref=ob.at[slot], dst_ref=rbo.at[slot], send_sem=o_s.at[0],
             recv_sem=o_r.at[slot], device_id={"req": grp}, device_id_type=MESH,
         ).wait_recv()
-        out[slot] = rbo[slot]
+    got = [rbo[g].astype(F32) for g in range(G)]
+    for c in range(out.shape[0]):
+        for q in range(N):
+            out[c, :, q * W:(q + 1) * W] = jnp.concatenate(
+                [x[4 * q + c:4 * q + c + 1] for x in got], axis=0
+            ).astype(BF16)
     for copy in sends:
         copy.wait_send()
 
@@ -341,7 +348,7 @@
     dma = pltpu.SemaphoreType.DMA
     out = pl.pallas_call(
         functools.partial(body, dims),
-        out_shape=jax.ShapeDtypeStruct((G, 8 * CH, W), BF16),
+        out_shape=jax.ShapeDtypeStruct((capacity, G, PF), BF16),
         in_specs=[vmem] * 10 + [hbm] * 3,
         out_specs=vmem,
         scratch_shapes=[
@@ -387,8 +394,7 @@
         tokens.reshape(C, R // C, D), segments, norm_gain, qk_gain, bproj, layer_scale,
         ln_weight, ln_bias, b_merge, owners[:, :, 0], wqkv, wproj, w_merge,
     )
-    slots = out.reshape(G, 2 * CH, 4, W).transpose(0, 2, 1, 3).reshape(G, 4, PF)
-    return slots[:, :capacity].reshape(1, G, 1, capacity, PF)
+    return out.transpose(1, 0, 2).reshape(1, G, 1, capacity, PF)
 
 
 def solution(mesh):

time: 81 us -> 79 us (0.975)
  Pallas kernels: 79.1 us -> 77.2 us
    pallas_call x1, Pallas kernels: 79.1 us -> 77.2 us  [per_device(): pl.pallas_call(functools.partial(body, dims), out_shape=jax.ShapeDtypeStr...]
    reshape x3 -> x0, local copies, waits for them, and re-layouts: 1.62 us -> none  [the longest x2 0.96 us: per_device(): slots = out.reshape(G, 2 * CH, 4, W).transpose(0, 2, 1, 3).reshape(G, 4, PF)]
    unnamed x0 -> x1, local copies, waits for them, and re-layouts: none -> 1.54 us
where the time goes in v3:
time: 79 us; the launch traced here: 78.8 us
  Pallas kernels  77.2 us (98%)
  local copies, waits for them, and re-layouts  1.54 us (2%)
    pallas_call x1, Pallas kernels, per_device(): pl.pallas_call(functools.partial(body, dims), out_shape=jax.ShapeDtypeStr...  77.2 us

profile of v3, /device:TPU:0, one launch (start us, length us, event | category | flops | bytes accessed | tf_op | source)
XLA Modules:
  0.0 78.8 jit_solution(12838484734933174819)
XLA Ops:
  0.0 77.2 %shard_map.127 = bf16[3,4,3072]{2,1,0:T(4,128)(2,1)} custom-call(bf16[2,16,3200]{2,1,0:T(8,128)(2,1)} %bitcast.6, s32[1,256]{1,0:T(1,128)} %segs.1, f32[3200]{0:T(1024)} %gain.1, f32[2,256]{1,0:T(2,128)} %qk_gain.1, f32[400]{0:T(512)} %bias.1, f32[400]{0:T(512)} %lscale.1, f32[4,400]{1,0:T(4,128)} %ln_w.1, f32[4,400]{1,0:T(4,128)} %ln_b.1, f32[3072]{0:T(1024)} %bm.1, ...), custom_call_target="tpu_custom_call" | custom-call | tf_op jit(solution)/shard_map/pallas_call | solution.py:349
  77.2 1.5 %copy.15 = bf16[1,4,1,3,3072]{4,1,3,2,0:T(4,128)(2,1)} copy(bf16[1,4,1,3,3072]{4,1,3,2,0:T(4,128)(2,1)} %bitcast.5) | data formatting | bytes 147456
